TPU v7x, 128 devices: a whole 4x4x4 slice. The times are simulated.
128 devices in a mesh: half: 2 (over z_lo), row: 8 (over x, z_hi), col: 8 (over y, core).
Axes of the slice: x: 4, y: 4, z: 4 (z_hi: 2, z_lo: 2; z = z_hi * 2 + z_lo), core: 2. Of those that a mesh axis runs over, the one named last changes fastest.
Arguments:
- child_pivot: float32 [2, 1024, 1024], P('half'), may hold values from 0 to 6, as said below
- child_border: float32 [2, 8, 8, 128, 1024], P('half', None, 'row'), may hold values from 0 to 6, as said below
- child_update: float32 [2, 8, 8, 128, 8, 8, 128], P('half', None, 'row', None, None, 'col'), may hold values from 0 to 6, as said below
- index_map: int32 [2, 64], replicated, may hold values from 0 to 79, as said below
- root_front: float32 [5, 16, 128, 10, 8, 128], P(None, ('half', 'row'), None, None, 'col'), may hold values from 0 to 6, as said below
Outputs:
- child_factor: float32 [2, 8, 8, 128, 1024], P('half', None, 'row')
- root_factor: float32 [5, 16, 128, 10, 8, 128], P(None, ('half', 'row'), None, None, 'col')
Inputs may be any that keep to these rules, and one draw needn't show every extreme that they name: `index_map`: for each sibling the entries are distinct; entry p gives the root block that receives update block p. Among the entries p of one sibling with equal p modulo the row axis's device count (a class), no residue modulo that count occurs more than 2 times, and in every class one residue occurs exactly 2 times; within a class no residue modulo twice that count occurs more than once; in particular the two entries sharing a residue differ modulo twice that count. child_pivot[s], child_border[s] and child_update[s] are the pivot, border and update blocks of one symmetric positive definite front of order 1024 + 8192; entries are not negative. `child_border`: the border block of the front described for child_pivot. `child_update`: the update block of the front described for child_pivot. `root_front`: symmetric positive definite; entries are not negative.
All inputs are finite; a program needn't handle non-finite values.
Results may differ from a plain program's by a relative error of at most 0.00012.
Values sent between devices are 32-bit elements; how exact they have to be, the bound alone decides.
No kernel may reach another device: no remote copies, remote signals or barrier semaphores. Data moves between devices by JAX's collectives and lax.ppermute only.
A program may use at most 192 MiB of HBM per device.

v0:
```python
import jax
import jax.numpy as jnp
from jax import lax
from jax.sharding import PartitionSpec as P

PANEL = 1024


precise = lax.Precision.HIGHEST


def broadcast(block, axis, owner):
    block = jnp.where(lax.axis_index(axis) == owner, block, jnp.zeros_like(block))
    return lax.psum(block, axis)


def solve_right(lower_factor, right_side):
    return lax.linalg.triangular_solve(
        lower_factor, right_side, left_side=False, lower=True, transpose_a=True
    )


def blocked_cholesky(matrix):
    whole_order = matrix.shape[0]
    half_order = whole_order // 2
    leading = jnp.linalg.cholesky(matrix[:half_order, :half_order])
    lower_left = solve_right(leading, matrix[half_order:, :half_order])
    schur_block = matrix[half_order:, half_order:] - jnp.dot(
        lower_left, lower_left.T, precision=precise
    )
    corner = jnp.linalg.cholesky(schur_block)
    upper_rows = jnp.concatenate(
        [leading, jnp.zeros((half_order, whole_order - half_order), jnp.float32)], axis=1
    )
    lower_part = jnp.concatenate([lower_left, corner], axis=1)
    return jnp.concatenate([upper_rows, lower_part], axis=0)


def place_codes(targets, buckets, capacity):
    onehot = (targets[..., None] == jnp.arange(buckets, dtype=jnp.int32)).astype(jnp.int32)
    earlier = jnp.cumsum(onehot, axis=-2) - onehot
    return targets * capacity + jnp.sum(onehot * earlier, axis=-1)


def pick_sources(slot_codes, slot_total):
    matches = (slot_codes[:, None] == jnp.arange(slot_total, dtype=jnp.int32)[None, :]).astype(
        jnp.int32
    )
    positions = jnp.arange(slot_codes.shape[0], dtype=jnp.int32)
    return jnp.sum(matches * positions[:, None], axis=0)


def collect(flat_index, arrive, target, slot_count):
    matches = jnp.logical_and(
        arrive[..., None], target[..., None] == jnp.arange(slot_count, dtype=jnp.int32)
    )
    matches = matches.astype(jnp.int32).reshape(-1, slot_count)
    picked = jnp.sum(matches * flat_index.reshape(-1, 1), axis=0)
    return (picked, jnp.sum(matches, axis=0).astype(jnp.float32))


def per_device(child_pivot, child_border, child_update, index_map, root_front):
    n_rows = lax.axis_size("row")
    n_cols = lax.axis_size("col")
    sibling = lax.axis_index("half")
    row_index = lax.axis_index("row")
    col_index = lax.axis_index("col")
    block_count = child_border.shape[1]
    block_size = child_border.shape[3]
    pivots = child_border.shape[4]
    local_rows = block_count * block_size
    root_rows = root_front.shape[0]
    root_cols = root_front.shape[3]
    root_width = root_cols * block_size
    capacity = block_count // n_rows + 1
    pivot_factor = blocked_cholesky(child_pivot[0])
    child_rows = solve_right(pivot_factor, child_border.reshape(local_rows, pivots))
    column_rows = broadcast(child_rows, "row", col_index)
    update = child_update.reshape(local_rows, local_rows) - jnp.dot(
        child_rows, column_rows.T, precision=precise
    )
    child_map = lax.dynamic_index_in_dim(index_map, sibling, 0, keepdims=False).reshape(
        block_count, n_rows
    )
    outgoing = lax.dynamic_index_in_dim(child_map, col_index, 1, keepdims=False)
    chosen = pick_sources(place_codes(outgoing % n_cols, n_cols, capacity), n_cols * capacity)
    sending = jnp.take(update.reshape(local_rows, block_count, block_size), chosen, axis=1)
    arrived = lax.all_to_all(
        sending.reshape(local_rows, n_cols, capacity, block_size),
        "col",
        split_axis=1,
        concat_axis=1,
        tiled=True,
    )
    source_map = child_map.T
    source_dest = source_map % n_cols
    source_rank = place_codes(source_dest, n_cols, capacity) - source_dest * capacity
    flat_index = jnp.arange(n_cols, dtype=jnp.int32)[:, None] * capacity + source_rank
    index_cols, present_cols = collect(
        flat_index, source_dest == col_index, source_map // n_cols, root_cols
    )
    placed = jnp.take(
        arrived.reshape(local_rows, n_cols * capacity, block_size), index_cols, axis=1
    )
    placed = (placed * present_cols[None, :, None]).reshape(block_count, block_size, root_width)
    outgoing_rows = lax.dynamic_index_in_dim(child_map, row_index, 1, keepdims=False)
    groups = 2 * n_rows
    joined_capacity = (capacity + 1) // 2
    chosen_rows = pick_sources(
        place_codes(outgoing_rows % groups, groups, joined_capacity), groups * joined_capacity
    )
    sending_rows = jnp.take(placed, chosen_rows, axis=0).reshape(
        groups, joined_capacity, block_size, root_width
    )
    arrived_rows = lax.all_to_all(
        sending_rows, ("half", "row"), split_axis=0, concat_axis=0, tiled=True
    )
    every_map = jnp.transpose(index_map.reshape(2, block_count, n_rows), (0, 2, 1))
    every_dest = every_map % groups
    every_rank = place_codes(every_dest, groups, joined_capacity) - every_dest * joined_capacity
    every_flat = (
        jnp.arange(groups, dtype=jnp.int32).reshape(2, n_rows, 1) * joined_capacity + every_rank
    )
    target_group = sibling * n_rows + row_index
    flat_rows = arrived_rows.reshape(groups * joined_capacity, block_size, root_width)
    contribution = jnp.zeros((root_rows, block_size, root_width), jnp.float32)
    for source_half in range(2):
        index_rows, present_rows = collect(
            every_flat[source_half],
            every_dest[source_half] == target_group,
            every_map[source_half] // groups,
            root_rows,
        )
        contribution = (
            contribution + jnp.take(flat_rows, index_rows, axis=0) * present_rows[:, None, None]
        )
    assembled = root_front.reshape(root_rows, block_size, root_width) + contribution
    panel_slots = PANEL // (block_size * n_cols)
    panel_blocks = PANEL // block_size
    own_panel = assembled.reshape(root_rows, 1, block_size, root_cols, 1, block_size)[
        :, :, :, :panel_slots
    ]
    panel_rows = lax.all_gather(own_panel, "col", axis=4, tiled=True).reshape(
        root_rows * block_size, PANEL
    )
    root_group = sibling * n_rows + row_index
    root_blocks = jnp.arange(root_rows, dtype=jnp.int32) * (2 * n_rows) + root_group
    selector = (root_blocks[:, None] == jnp.arange(panel_blocks, dtype=jnp.int32)[None, :]).astype(
        jnp.float32
    )
    panel_blocked = panel_rows.reshape(root_rows, 1, block_size, PANEL)
    top_part = jnp.sum(selector[:, :, None, None] * panel_blocked, axis=0)
    diagonal = lax.psum(top_part, ("half", "row")).reshape(PANEL, PANEL)
    root_pivot = blocked_cholesky(diagonal)
    solved = solve_right(root_pivot, panel_rows)
    pivot_index = jnp.clip(root_blocks, 0, panel_blocks - 1)
    pivot_rows = jnp.take(
        root_pivot.reshape(panel_blocks, block_size, PANEL), pivot_index, axis=0
    ).reshape(root_rows * block_size, PANEL)
    global_rows = (
        root_blocks[:, None] * block_size + jnp.arange(block_size, dtype=jnp.int32)[None, :]
    ).reshape(-1)
    is_top = global_rows < PANEL
    factor_rows = jnp.where(is_top[:, None], pivot_rows, solved)
    shared_rows = broadcast(factor_rows, "row", col_index)
    both_halves = lax.all_gather(
        shared_rows.reshape(root_rows, 1, block_size, PANEL), "half", axis=1, tiled=True
    )
    column_factor = both_halves.reshape(root_cols * block_size, PANEL)
    trailing = assembled.reshape(root_rows * block_size, root_width) - jnp.dot(
        factor_rows, column_factor.T, precision=precise
    )
    panel_part = lax.dynamic_index_in_dim(
        factor_rows.reshape(-1, panel_slots, n_cols, block_size), col_index, 2, keepdims=False
    )
    remainder = jnp.where(is_top[:, None], 0.0, trailing[:, panel_slots * block_size :])
    combined = jnp.concatenate(
        [panel_part.reshape(-1, panel_slots * block_size), remainder], axis=1
    )
    return (child_rows.reshape(child_border.shape), combined.reshape(root_front.shape))


def solution(mesh):
    in_specs = (
        P("half", None, None),
        P("half", None, "row", None, None),
        P("half", None, "row", None, None, "col", None),
        P(),
        P(None, ("half", "row"), None, None, "col", None),
    )
    out_specs = (
        P("half", None, "row", None, None),
        P(None, ("half", "row"), None, None, "col", None),
    )
    return jax.shard_map(
        per_device, mesh=mesh, in_specs=in_specs, out_specs=out_specs, check_vma=False
    )
```

profile of v0, /device:TPU:1, one launch (start us, length us, event | category | flops | bytes accessed | tf_op | source)
XLA Modules:
  0.0 1751.7 jit_solution(4113997298887584079)
XLA Ops:
  15.7 11.7 cholesky.462
  38.0 11.7 cholesky.481
  60.5 11.7 cholesky.502
  83.4 11.7 cholesky.519
  122.2 39.3 %custom-call.44 = f32[4,128,128]{1,2,0:T(8,128)S(1)} custom-call(f32[4,128,128]{2,1,0:T(8,128)S(1)} %get-tuple-element.35), custom_call_target="InvertDiagBlocksLowerTriangular" | custom-call | tf_op jit(solution)/shard_map/triangular_solve/custom-call.3 | solution.py:18
  203.9 13.2 cholesky.553
  274.3 23.2 %while.6 = (s32[]{:T(128)}, f32[1024,1024]{1,0:T(8,128)}, s32[8,2]{0,1:T(2,128)S(1)}, f32[8,128,128]{2,1,0:T(8,128)S(1)}, s32[]{:T(128)}) while((s32[]{:T(128)}, f32[1024,1024]{1,0:T(8,128)}, s32[8,2]{0,1:T(2,128)S(1)}, f32[8,128,128]{2,1,0:T(8,128)S(1)}, s32[]{:T(128)}) %tuple.166), condition=%wide.while_cond.1, body=%wide.while_body.1.sunk | while | flops 2 | bytes 131181 | solution.py:18
  297.5 78.8 %custom-call.29 = f32[8,128,128]{1,2,0:T(8,128)S(1)} custom-call(f32[8,128,128]{2,1,0:T(8,128)S(1)} %get-tuple-element.20), custom_call_target="InvertDiagBlocksLowerTriangular" | custom-call | tf_op jit(solution)/shard_map/triangular_solve | solution.py:18
  424.5 178.6 %all-reduce.7.cloned.1.call-done = f32[1024,1024]{1,0:T(8,128)} async-done(((f32[1024,1024]{1,0:T(8,128)}), f32[1024,1024]{1,0:T(8,128)}) %all-reduce.7.cloned.1.call-update) | async-done | bytes 4194320 | tf_op jit(solution)/shard_map/psum | solution.py:14
  603.0 18.5 %convolution_subtract_fusion = f32[1024,1024]{0,1:T(8,128)} fusion(f32[1024,1024]{0,1:T(8,128)} %copy.429, f32[1024,1024]{1,0:T(8,128)} %convolution_dynamic-update-slice_fusion, f32[1024,1024]{1,0:T(8,128)} %all-reduce.7.cloned.1.call-done), kind=kOutput, calls=%fused_computation.47 | convolution fusion | flops 12885950464 | bytes 16777216 | tf_op jit(solution)/shard_map/dot_general | solution.py:79
  651.8 92.4 %all-to-all-done = f32[1024,8,2,128]{3,0,2,1:T(8,128)} async-done(((f32[1024,8,2,128]{3,0,2,1:T(8,128)}), f32[1024,8,2,128]{3,0,2,1:T(8,128)}, u32[]{:S(2)}, u32[]{:S(2)}) %all-to-all-start) | async-done | bytes 8388640 | tf_op jit(solution)/shard_map/all_to_all | solution.py:88
  816.2 155.4 %all-to-all-done.1 = f32[16,1,128,1280]{3,2,1,0:T(8,128)} async-done(((f32[16,1,128,1280]{3,2,1,0:T(8,128)}), f32[16,1,128,1280]{3,2,1,0:T(8,128)}, u32[]{:S(2)}, u32[]{:S(2)}) %all-to-all-start.1) | async-done | bytes 10485792 | tf_op jit(solution)/shard_map/all_to_all | solution.py:115
  996.2 30.0 %all-gather.3.cloned.1.call-done = f32[5,1,128,1,8,128]{5,2,3,1,0,4:T(8,128)} async-done(((f32[5,1,128,1,1,128]{5,2,3,1,0,4:T(8,128)}), f32[5,1,128,1,8,128]{5,2,3,1,0,4:T(8,128)}) %all-gather.3.cloned.1.call-update) | async-done | bytes 2621456 | tf_op jit(solution)/shard_map/all_gather | solution.py:143
  1045.7 98.4 %all-reduce.9.cloned.1.call-done = f32[1024,1024]{0,1:T(8,128)} async-done(((f32[1024,1024]{0,1:T(8,128)}), f32[1024,1024]{0,1:T(8,128)}) %all-reduce.9.cloned.1.call-update) | async-done | bytes 4194320 | tf_op jit(solution)/shard_map/psum | solution.py:153
  1147.2 11.7 cholesky.606
  1169.6 12.1 cholesky.625
  1193.6 11.7 cholesky.646
  1216.4 11.9 cholesky.663
  1240.4 39.3 %custom-call.51 = f32[4,128,128]{1,2,0:T(8,128)S(1)} custom-call(f32[4,128,128]{2,1,0:T(8,128)S(1)} %get-tuple-element.36), custom_call_target="InvertDiagBlocksLowerTriangular" | custom-call | tf_op jit(solution)/shard_map/triangular_solve/custom-call.3 | solution.py:18
  1388.6 24.0 %while.7 = (s32[]{:T(128)}, f32[1024,1024]{1,0:T(8,128)}, s32[8,2]{0,1:T(2,128)S(1)}, f32[8,128,128]{2,1,0:T(8,128)S(1)}, s32[]{:T(128)}) while((s32[]{:T(128)}, f32[1024,1024]{1,0:T(8,128)}, s32[8,2]{0,1:T(2,128)S(1)}, f32[8,128,128]{2,1,0:T(8,128)S(1)}, s32[]{:T(128)}) %tuple.185), condition=%wide.while_cond.2, body=%wide.while_body.2.sunk | while | flops 2 | bytes 131181 | solution.py:18
  1412.6 79.4 %custom-call.30 = f32[8,128,128]{1,2,0:T(8,128)} custom-call(f32[8,128,128]{2,1,0:T(8,128)S(1)} %get-tuple-element.28), custom_call_target="InvertDiagBlocksLowerTriangular" | custom-call | tf_op jit(solution)/shard_map/triangular_solve | solution.py:18
  1524.0 126.1 %all-reduce.11.cloned.1.call-done = f32[5,1,128,1024]{3,2,1,0:T(8,128)} async-done(((f32[5,1,128,1024]{3,2,1,0:T(8,128)}), f32[5,1,128,1024]{3,2,1,0:T(8,128)}) %all-reduce.11.cloned.1.call-update) | async-done | bytes 2621456 | tf_op jit(solution)/shard_map/psum | solution.py:14
  1660.6 65.2 %all-gather.5.cloned.1.call-done = f32[5,2,128,1024]{3,2,1,0:T(8,128)} async-done(((f32[5,1,128,1024]{3,2,1,0:T(8,128)}), f32[5,2,128,1024]{3,2,1,0:T(8,128)}) %all-gather.5.cloned.1.call-update) | async-done | bytes 5242896 | tf_op jit(solution)/shard_map/all_gather | solution.py:166
  1725.8 13.1 fusion.217
  (423 shorter events, 622.9 us)
Async XLA Ops:
  7.2 595.9 %all-reduce.7.cloned.1.call-start = ((), (), s32[]{:S(2)}) async-start(), calls=%async_computation.2 | async-start | bytes 8388608 | tf_op jit(solution)/shard_map/psum | solution.py:14
  380.3 2.4 copy-start.6
  417.5 5.4 copy-start.21
  644.6 99.6 %all-to-all-start = ((f32[1024,8,2,128]{3,0,2,1:T(8,128)}), f32[1024,8,2,128]{3,0,2,1:T(8,128)}, u32[]{:S(2)}, u32[]{:S(2)}) async-start(f32[1024,8,2,128]{3,0,2,1:T(8,128)} %broadcast_select_fusion), calls=%async_computation | async-start | bytes 16777216 | tf_op jit(solution)/shard_map/all_to_all | solution.py:88
  789.6 10.3 copy-start.5
  789.7 181.9 %all-to-all-start.1 = ((f32[16,1,128,1280]{3,2,1,0:T(8,128)}), f32[16,1,128,1280]{3,2,1,0:T(8,128)}, u32[]{:S(2)}, u32[]{:S(2)}) async-start(f32[16,1,128,1280]{3,2,1,0:T(8,128)} %fusion), calls=%async_computation.1 | async-start | bytes 20971520 | tf_op jit(solution)/shard_map/all_to_all | solution.py:115
  797.6 228.5 %all-gather.3.cloned.1.call-start = ((), (), s32[]{:S(2)}) async-start(), calls=%async_computation.3 | async-start | bytes 2949120 | tf_op jit(solution)/shard_map/all_gather | solution.py:143
  989.1 3.4 copy-start
  996.0 148.1 %all-reduce.9.cloned.1.call-start = ((), (), s32[]{:S(2)}) async-start(), calls=%async_computation.4 | async-start | bytes 8388608 | tf_op jit(solution)/shard_map/psum | solution.py:153
  1040.4 1.7 copy-start.3
  1040.4 609.7 %all-reduce.11.cloned.1.call-start = ((), (), s32[]{:S(2)}) async-start(), calls=%async_computation.5 | async-start | bytes 5242880 | tf_op jit(solution)/shard_map/psum | solution.py:14
  1292.3 1.0 copy-start.10
  1381.8 110.2 %copy-start.4 = (f32[80,8,8,128]{3,1,2,0:T(8,128)S(1)}, f32[80,8,8,128]{3,1,2,0:T(8,128)}, u32[]{:S(2)}) copy-start(f32[80,8,8,128]{3,1,2,0:T(8,128)} %copy.440) | copy-start | bytes 7864324
  1492.1 5.5 copy-start.19
  1498.1 5.9 copy-start.7
  1500.5 5.9 copy-start.13
  1515.9 1.5 copy-start.2
  1524.0 201.8 %all-gather.5.cloned.1.call-start = ((), (), s32[]{:S(2)}) async-start(), calls=%async_computation.6 | async-start | bytes 7864320 | tf_op jit(solution)/shard_map/all_gather | solution.py:166
  1652.5 1.1 copy-start.14
  1652.5 1.2 copy-start.15
  1652.5 1.2 copy-start.17
  1653.1 1.1 copy-start.18
  1653.1 1.2 copy-start.16
  1725.8 13.1 copy-start.1
  (5 other events, 4.3 us)
Sparse Core Ops, SparseCore 0:
  412.5 190.5 all-reduce.6
  996.1 29.9 all-gather.2
  1040.5 103.5 all-reduce.8
  1524.1 125.9 all-reduce.10
  1651.6 74.1 all-gather.4
where the time goes:
time: 1760 us; the launch traced here: 1750 us
  waiting for transfers between devices  746 us (42%)
  other arithmetic  643 us (37%)
  local copies, waits for them, and re-layouts  197 us (11%)
  matrix products  125 us (7%)
  between operations  25.8 us (1%)
    psum x2, waiting for transfers between devices, broadcast(): return lax.psum(block, axis)  305 us
    another operation x9, other arithmetic, solve_right(): lax.linalg.triangular_solve(lower_factor, right_side, left_side=False, lo...  254 us
    another operation x30, other arithmetic, blocked_cholesky(): corner = jnp.linalg.cholesky(schur_block)  162 us
    another operation x29, other arithmetic, blocked_cholesky(): leading = jnp.linalg.cholesky(matrix[:half_order, :half_order])  158 us
    all_to_all x1, waiting for transfers between devices, per_device(): lax.all_to_all(sending_rows, ('half', 'row'), split_axis=0, concat_axis=0...  155 us
    psum x1, waiting for transfers between devices, per_device(): diagonal = lax.psum(top_part, ('half', 'row')).reshape(PANEL, PANEL)  98.4 us
    all_to_all x1, waiting for transfers between devices, per_device(): lax.all_to_all(sending.reshape(local_rows, n_cols, capacity, block_size),...  92.4 us
    another operation x44, matrix products, solve_right(): lax.linalg.triangular_solve(lower_factor, right_side, left_side=False, lo...  71.9 us
  transfers between devices with their start and end apart: 7, of which 7 were waited for; matrix products, arithmetic and copies ran while one was open for 3% of the time, Pallas kernels for 0%

commit v1 on v0

v1 whole, which is shorter than its diff:
```python
import functools

import jax
import jax.numpy as jnp
from jax import lax
from jax.experimental import pallas as pl
from jax.experimental.pallas import tpu as pltpu
from jax.sharding import PartitionSpec as P

PANEL = 1024
BLOCK = 128
STRIP = 32
F32 = jnp.float32
BF16 = jnp.bfloat16

exact = lax.Precision.HIGHEST
close = lax.Precision.HIGH


def split_three(values):
    high = values.astype(BF16)
    rest = values - high.astype(F32)
    middle = rest.astype(BF16)
    low = (rest - middle.astype(F32)).astype(BF16)
    return high, middle, low


def gram_strip(rows):
    high, middle, low = split_three(rows)
    left = jnp.concatenate([high, high, middle, high, middle, low], axis=0)
    right = jnp.concatenate([high, middle, high, low, middle, high], axis=0)
    return lax.dot_general(left, right, (((0,), (0,)), ((), ())), preferred_element_type=F32)


def inverse_root(pivot):
    guess = lax.rsqrt(pivot)
    return guess * (1.5 - 0.5 * pivot * guess * guess)


def eliminate_strip(rows, start):
    lanes = lax.broadcasted_iota(jnp.int32, (STRIP, BLOCK), 1)
    sublanes = lax.broadcasted_iota(jnp.int32, (STRIP, BLOCK), 0)
    columns = [
        jnp.broadcast_to(rows[:, start + j : start + j + 1], (STRIP, BLOCK)) for j in range(STRIP)
    ]
    inside = jnp.logical_and(lanes >= start, lanes < start + STRIP)
    rows = jnp.where(inside, jnp.where(lanes - start == sublanes, 1.0, 0.0), rows)
    for j in range(STRIP):
        scale = inverse_root(jnp.broadcast_to(columns[j][j : j + 1, :], (8, BLOCK)))
        factor = columns[j] * jnp.concatenate([scale] * (STRIP // 8), axis=0)
        for k in range(j + 1, STRIP):
            columns[k] = columns[k] - factor * jnp.broadcast_to(
                factor[k : k + 1, :], (STRIP, BLOCK)
            )
        solved = jnp.broadcast_to(rows[j : j + 1, :] * scale[0:1, :], (STRIP, BLOCK))
        rows = jnp.where(
            sublanes == j, solved, rows - jnp.where(sublanes > j, factor, 0.0) * solved
        )
    return rows


def eliminate_block(block):
    for start in range(0, BLOCK, STRIP):
        stop = start + STRIP
        rows = eliminate_strip(block[start:stop, :], start)
        block[start:stop, :] = rows
        if stop < BLOCK:
            change = gram_strip(rows)[stop:, :]
            lanes = lax.broadcasted_iota(jnp.int32, (BLOCK - stop, BLOCK), 1)
            inside = jnp.logical_and(lanes >= start, lanes < stop)
            block[stop:, :] = jnp.where(inside, 0.0, block[stop:, :]) - change


def inverse_factor_kernel(matrix, state, block, scaled):
    count = matrix.shape[0] // BLOCK
    state[...] = matrix[...]
    row_ids = lax.broadcasted_iota(jnp.int32, (BLOCK, BLOCK), 0)
    col_ids = lax.broadcasted_iota(jnp.int32, (BLOCK, BLOCK), 1)

    def step(j, _):
        here = pl.ds(pl.multiple_of(j * BLOCK, BLOCK), BLOCK)
        block[...] = state[here, here]
        eliminate_block(block)
        inverse = jnp.where(col_ids <= row_ids, block[...], 0.0)
        state[here, here] = jnp.where(col_ids == row_ids, 1.0, 0.0).astype(F32)
        scaled[...] = jnp.dot(
            inverse, state[here, :], precision=exact, preferred_element_type=F32
        )
        state[here, :] = scaled[...]

        def update(i, _):
            there = pl.ds(pl.multiple_of(i * BLOCK, BLOCK), BLOCK)
            state[there, here] = jnp.zeros((BLOCK, BLOCK), F32)
            state[there, :] = state[there, :] - lax.dot_general(
                scaled[:, there],
                scaled[...],
                (((0,), (0,)), ((), ())),
                precision=exact,
                preferred_element_type=F32,
            )
            return 0

        lax.fori_loop(j + 1, count, update, 0)
        return 0

    lax.fori_loop(0, count, step, 0)

    def clear(i, _):
        here = pl.ds(pl.multiple_of(i * BLOCK, BLOCK), BLOCK)

        def clear_block(k, _):
            right = pl.ds(pl.multiple_of(k * BLOCK, BLOCK), BLOCK)
            state[here, right] = jnp.zeros((BLOCK, BLOCK), F32)
            return 0

        lax.fori_loop(i + 1, count, clear_block, 0)
        return 0

    lax.fori_loop(0, count, clear, 0)


def inverse_factor(matrix):
    order = matrix.shape[0]
    whole = pl.BlockSpec(memory_space=pltpu.VMEM)
    return pl.pallas_call(
        inverse_factor_kernel,
        out_shape=jax.ShapeDtypeStruct((order, order), F32),
        in_specs=[whole],
        out_specs=whole,
        scratch_shapes=[pltpu.VMEM((BLOCK, BLOCK), F32), pltpu.VMEM((BLOCK, order), F32)],
        compiler_params=pltpu.CompilerParams(vmem_limit_bytes=32 * 1024 * 1024),
        cost_estimate=pl.CostEstimate(
            flops=60_000_000_000, bytes_accessed=8 * order * order, transcendentals=0
        ),
        name="inverse_factor",
    )(matrix)


def spread_kernel(slots, source, target):
    blocks = source.shape[0] // target.shape[1]
    for b in range(blocks):
        target[slots[b]] = source[pl.ds(b, target.shape[1], stride=blocks), :]


def spread_columns(slots, source, slot_total, blocks):
    rows = source.shape[0] // blocks
    tile = rows // 4
    return pl.pallas_call(
        spread_kernel,
        out_shape=jax.ShapeDtypeStruct((slot_total, rows, BLOCK), F32),
        grid_spec=pltpu.PrefetchScalarGridSpec(
            num_scalar_prefetch=1,
            grid=(4,),
            in_specs=[pl.BlockSpec((tile * blocks, BLOCK), lambda i, s: (i, 0))],
            out_specs=pl.BlockSpec((slot_total, tile, BLOCK), lambda i, s: (0, i, 0)),
        ),
        compiler_params=pltpu.CompilerParams(vmem_limit_bytes=32 * 1024 * 1024),
        cost_estimate=pl.CostEstimate(
            flops=0, bytes_accessed=4 * BLOCK * rows * (blocks + slot_total), transcendentals=0
        ),
        name="spread_columns",
    )(slots, source)


def ranks(targets):
    same = targets[..., :, None] == targets[..., None, :]
    length = targets.shape[-1]
    earlier = jnp.arange(length)[:, None] > jnp.arange(length)[None, :]
    return jnp.sum(jnp.logical_and(same, earlier).astype(jnp.int32), axis=-1)


def locate(matches, values):
    matches = matches.astype(jnp.int32)
    return (jnp.sum(matches * values, axis=-1), jnp.sum(matches, axis=-1) > 0)


def times_transposed(left, right, precision):
    return lax.dot_general(
        left, right, (((1,), (1,)), ((), ())), precision=precision, preferred_element_type=F32
    )


def per_device(child_pivot, child_border, child_update, index_map, root_front):
    n_rows = lax.axis_size("row")
    n_cols = lax.axis_size("col")
    groups = 2 * n_rows
    sibling = lax.axis_index("half")
    row_index = lax.axis_index("row")
    col_index = lax.axis_index("col")
    group = sibling * n_rows + row_index
    block_count = child_border.shape[1]
    pivots = child_border.shape[4]
    local_rows = block_count * BLOCK
    root_rows = root_front.shape[0]
    root_cols = root_front.shape[3]
    capacity = 2
    numbers = jnp.arange(block_count, dtype=jnp.int32)

    child_map = lax.dynamic_index_in_dim(index_map, sibling, 0, keepdims=False).reshape(
        block_count, n_rows
    )
    by_class = child_map.T
    class_dest = by_class % n_cols
    class_rank = ranks(class_dest)
    col_dest = lax.dynamic_index_in_dim(class_dest, col_index, 0, keepdims=False)
    col_rank = lax.dynamic_index_in_dim(class_rank, col_index, 0, keepdims=False)
    row_map = lax.dynamic_index_in_dim(by_class, row_index, 0, keepdims=False)
    row_dest = lax.dynamic_index_in_dim(class_dest, row_index, 0, keepdims=False)
    row_rank = lax.dynamic_index_in_dim(class_rank, row_index, 0, keepdims=False)

    border = child_border.reshape(block_count, BLOCK, pivots)
    wanted, _ = locate(
        jnp.logical_and(
            row_dest[None, :] == col_index,
            row_rank[None, :] == jnp.arange(capacity, dtype=jnp.int32)[:, None],
        ),
        numbers,
    )
    own_wanted = jnp.take(border, wanted, axis=0)
    every_wanted = lax.all_gather(own_wanted, "row", axis=0, tiled=True)

    sending = spread_columns(
        col_dest * capacity + col_rank,
        child_update.reshape(local_rows * block_count, BLOCK),
        n_cols * capacity,
        block_count,
    )
    arrived = lax.all_to_all(sending, "col", split_axis=0, concat_axis=0, tiled=True)

    flat_source = numbers[:, None] * capacity + class_rank
    wanted_roots = jnp.arange(root_cols, dtype=jnp.int32) * n_cols + col_index
    source_slots, source_there = locate(
        by_class.reshape(1, -1) == wanted_roots[:, None], flat_source.reshape(-1)
    )

    inverse = inverse_factor(child_pivot[0])
    own_factor = times_transposed(border.reshape(local_rows, pivots), inverse, exact)
    column_border = jnp.take(every_wanted, source_slots, axis=0)
    column_update = jnp.take(arrived, source_slots, axis=0)

    def schur(first, last):
        count = last - first
        factor = times_transposed(
            column_border[first:last].reshape(count * BLOCK, pivots), inverse, exact
        )
        product = lax.dot_general(
            factor.reshape(count, BLOCK, pivots),
            own_factor,
            (((2,), (1,)), ((), ())),
            precision=close,
            preferred_element_type=F32,
        )
        product = jnp.transpose(product, (0, 2, 1))
        there = source_there[first:last, None, None]
        return jnp.where(there, column_update[first:last] - product, 0.0).reshape(
            count, block_count, BLOCK, BLOCK
        )

    panel_update = schur(0, 1)[0]
    root_view = root_front.reshape(root_rows, BLOCK, root_cols, BLOCK)

    top_index, top_there = locate(row_map[None, :] == numbers[:, None], numbers)
    top_part = jnp.where(top_there[:, None, None], jnp.take(panel_update, top_index, axis=0), 0.0)
    is_owner = jnp.logical_and(sibling == 0, row_index == numbers)
    top_part = top_part + jnp.where(is_owner[:, None, None], root_view[0, :, 0, :][None], 0.0)
    leading_cols = lax.psum(top_part, ("half", "row")).reshape(PANEL, BLOCK)
    leading = lax.all_gather(leading_cols, "col", axis=1, tiled=True)

    sent_blocks, _ = locate(
        (row_map % groups)[None, :] == jnp.arange(groups, dtype=jnp.int32)[:, None], numbers
    )
    every_map = index_map.reshape(2, 1, block_count * n_rows)
    my_roots = jnp.arange(root_rows, dtype=jnp.int32) * groups + group
    sender = (
        jnp.arange(2, dtype=jnp.int32)[:, None, None] * n_rows
        + (jnp.arange(block_count * n_rows, dtype=jnp.int32) % n_rows)[None, None, :]
    )
    got_slots, got_there = locate(every_map == my_roots[None, :, None], sender)

    def extend_add(base, received):
        shape = (-1,) + (1,) * (received.ndim - 1)
        for half in range(2):
            picked = jnp.take(received, got_slots[half], axis=0)
            base = base + jnp.where(got_there[half].reshape(shape), picked, 0.0)
        return base

    panel_sent = jnp.take(panel_update, sent_blocks, axis=0)
    panel_got = lax.all_to_all(
        panel_sent, ("half", "row"), split_axis=0, concat_axis=0, tiled=True
    )
    own_panel = extend_add(root_view[:, :, 0, :], panel_got)
    panel_rows = lax.all_gather(own_panel, "col", axis=2, tiled=True)
    swaps = [(r * n_cols + c, c * n_rows + r) for r in range(n_rows) for c in range(n_cols)]
    swapped = lax.ppermute(own_panel, ("row", "col"), swaps)
    column_panel = lax.all_gather(swapped, ("half", "row"), axis=0, tiled=False).reshape(
        2, n_rows, root_rows, BLOCK, BLOCK
    )
    column_panel = jnp.transpose(column_panel, (2, 0, 3, 1, 4)).reshape(root_cols, BLOCK, PANEL)

    rest_update = schur(1, root_cols)
    rest_sent = jnp.take(jnp.transpose(rest_update, (1, 0, 2, 3)), sent_blocks, axis=0)
    rest_got = lax.all_to_all(rest_sent, ("half", "row"), split_axis=0, concat_axis=0, tiled=True)

    root_inverse = inverse_factor(leading)
    factor_rows = times_transposed(panel_rows.reshape(root_rows * BLOCK, PANEL), root_inverse, exact)
    column_factor = times_transposed(
        column_panel[1:].reshape((root_cols - 1) * BLOCK, PANEL), root_inverse, exact
    )
    global_rows = (
        my_roots[:, None] * BLOCK + jnp.arange(BLOCK, dtype=jnp.int32)[None, :]
    ).reshape(-1)
    is_top = global_rows < PANEL
    above = jnp.logical_and(
        is_top[:, None], jnp.arange(PANEL, dtype=jnp.int32)[None, :] > global_rows[:, None]
    )
    factor_rows = jnp.where(above, 0.0, factor_rows)
    rest = jnp.transpose(root_view[:, :, 1:, :], (0, 2, 1, 3))
    rest = extend_add(rest, rest_got)
    trailing = jnp.transpose(rest, (0, 2, 1, 3)).reshape(
        root_rows * BLOCK, -1
    ) - times_transposed(factor_rows, column_factor, close)
    panel_part = lax.dynamic_index_in_dim(
        factor_rows.reshape(-1, n_cols, BLOCK), col_index, 1, keepdims=False
    )
    remainder = jnp.where(is_top[:, None], 0.0, trailing)
    combined = jnp.concatenate([panel_part, remainder], axis=1)
    return (own_factor.reshape(child_border.shape), combined.reshape(root_front.shape))


def solution(mesh):
    in_specs = (
        P("half", None, None),
        P("half", None, "row", None, None),
        P("half", None, "row", None, None, "col", None),
        P(),
        P(None, ("half", "row"), None, None, "col", None),
    )
    out_specs = (
        P("half", None, "row", None, None),
        P(None, ("half", "row"), None, None, "col", None),
    )
    return jax.shard_map(
        per_device, mesh=mesh, in_specs=in_specs, out_specs=out_specs, check_vma=False
    )
```

time: 1760 us -> 642 us (0.36)
  the two profiles are of different devices: /device:TPU:1 before, /device:TPU:42 now
where the time goes in v1:
time: 642 us; the launch traced here: 632 us
  waiting for transfers between devices  289 us (45%)
  Pallas kernels  103 us (16%)
  matrix products  89.3 us (14%)
  local copies, waits for them, and re-layouts  83 us (13%)
  other arithmetic  29.7 us (5%)
  starting transfers between devices  23.5 us (4%)
  between operations  14.9 us (2%)
    all_to_all x1, waiting for transfers between devices, per_device(): lax.all_to_all(rest_sent, ('half', 'row'), split_axis=0, concat_axis=0, t...  116 us
    pallas_call x2, Pallas kernels, inverse_factor(): pl.pallas_call(inverse_factor_kernel, out_shape=jax.ShapeDtypeStruct((ord...  101 us
    psum x1, waiting for transfers between devices, per_device(): leading_cols = lax.psum(top_part, ('half', 'row')).reshape(PANEL, BLOCK)  84.8 us
    dot_general x6, matrix products, times_transposed(): lax.dot_general(left, right, (((1,), (1,)), ((), ())), precision=precisio...  75.8 us
    all_gather x1, waiting for transfers between devices, per_device(): lax.all_gather(swapped, ('half', 'row'), axis=0, tiled=False)  52.5 us
    all_to_all x1, waiting for transfers between devices, per_device(): lax.all_to_all(sending, 'col', split_axis=0, concat_axis=0, tiled=True)  21.6 us
    unnamed x50, local copies, waits for them, and re-layouts  17 us
    dot_general x2, matrix products, schur(): lax.dot_general(factor.reshape(count, BLOCK, pivots), own_factor, (((2,),...  13.6 us
  transfers between devices with their start and end apart: 9, of which 5 were waited for; matrix products, arithmetic and copies ran while one was open for 18% of the time, Pallas kernels for 16%

profile of v1, /device:TPU:42, one launch (start us, length us, event | category | flops | bytes accessed | tf_op | source)
XLA Modules:
  0.0 632.3 jit_solution(3892279274396615581)
XLA Ops:
  20.1 5.6 all-to-all-start
  29.8 50.7 %inverse_factor.2 = f32[1024,1024]{1,0:T(8,128)S(1)} custom-call(f32[1024,1024]{1,0:T(8,128)S(1)} %bitcast.111), custom_call_target="tpu_custom_call" | custom-call | flops 60000002048 | bytes 8388608 | tf_op jit(solution)/shard_map/inverse_factor/pallas_call | solution.py:125
  82.4 14.9 %fusion.40 = f32[1024,1024]{1,0:T(8,128)} fusion(f32[1024,1024]{1,0:T(8,128)S(1)} %bitcast.131, f32[1024,1024]{1,0:T(8,128)S(1)} %inverse_factor.2), kind=kOutput, calls=%fused_computation.133 | convolution fusion | flops 12884901888 | bytes 12582912 | tf_op jit(solution)/shard_map/dot_general | solution.py:178
  97.3 21.6 %all-to-all-done = f32[16,1024,128]{2,1,0:T(8,128)} async-done(((f32[16,1024,128]{2,1,0:T(8,128)}), f32[16,1024,128]{2,1,0:T(8,128)}, u32[]{:S(2)}, u32[]{:S(2)}) %all-to-all-start) | async-done | bytes 8388640 | tf_op jit(solution)/shard_map/all_to_all | solution.py:228
  119.0 6.6 %gather_fusion = f32[10,1024,128]{2,1,0:T(8,128)} fusion(f32[16,1024,128]{2,1,0:T(8,128)} %all-to-all-done, s32[1024]{0:T(1024)S(1)} %pad_clamp_fusion.5), kind=kCustom, calls=%fused_computation.4 | custom fusion | bytes 10485800 | tf_op jit(solution)/shard_map/jit(_take)/gather | solution.py:239
  130.8 6.7 %gather_fusion.2 = f32[10,128,1024]{2,1,0:T(8,128)} fusion(f32[16,128,1024]{2,1,0:T(8,128)} %all-gather.6.cloned.1.call-done, s32[1024]{0:T(1024)S(1)} %pad_clamp_fusion.5), kind=kCustom, calls=%fused_computation.6 | custom fusion | bytes 10485800 | tf_op jit(solution)/shard_map/jit(_take)/gather | solution.py:238
  150.3 84.8 %all-reduce.2.cloned.1.call-done = f32[1024,128]{1,0:T(8,128)} async-done(((f32[1024,128]{1,0:T(8,128)}), f32[1024,128]{1,0:T(8,128)}) %all-reduce.2.cloned.1.call-update) | async-done | bytes 524304 | tf_op jit(solution)/shard_map/psum | solution.py:266
  237.6 7.0 %all-to-all-start.1 = ((f32[16,128,128]{2,1,0:T(8,128)}), f32[16,128,128]{2,1,0:T(8,128)S(1)}, u32[]{:S(2)}, u32[]{:S(2)}) async-start(f32[16,128,128]{2,1,0:T(8,128)} %broadcast_select_fusion.3), calls=%async_computation.1 | async-start | bytes 2097152 | tf_op jit(solution)/shard_map/all_to_all | solution.py:288
  244.9 13.5 %all-to-all-done.1 = f32[16,128,128]{2,1,0:T(8,128)S(1)} async-done(((f32[16,128,128]{2,1,0:T(8,128)}), f32[16,128,128]{2,1,0:T(8,128)S(1)}, u32[]{:S(2)}, u32[]{:S(2)}) %all-to-all-start.1) | async-done | bytes 1048608 | tf_op jit(solution)/shard_map/all_to_all | solution.py:288
  261.7 18.9 %fusion.3 = f32[9,128,1024]{2,1,0:T(8,128)S(1)} fusion(f32[10,128,1024]{2,1,0:T(8,128)} %copy-done.13, f32[1024,1024]{1,0:T(8,128)} %copy-done.1), kind=kOutput, calls=%fused_computation.15 | convolution fusion | flops 14495514624 | bytes 14155776 | tf_op jit(solution)/shard_map/dot_general | solution.py:178
  281.3 10.6 %fusion = f32[9,1024,128]{2,1,0:T(8,128)} fusion(f32[10,1024,128]{2,1,0:T(8,128)S(1)} %bitcast.114, pred[9]{0:T(512)(128)(4,1)S(1)} %slice.56, f32[9,128,1024]{2,1,0:T(8,128)S(1)} %fusion.3, f32[1024,1024]{1,0:T(8,128)S(1)} %copy-done.8), kind=kOutput, calls=%fused_computation.11 | convolution fusion | flops 7250116608 | bytes 18350088 | tf_op jit(solution)/shard_map/dot_general | solution.py:246
  291.9 7.3 %gather_fusion.5 = f32[16,9,128,128]{3,2,1,0:T(8,128)} fusion(f32[8,9,128,128]{3,2,0,1:T(8,128)} %bitcast.112, s32[1024]{0:T(1024)S(1)} %pad_clamp_fusion.3), kind=kCustom, calls=%fused_computation.9 | custom fusion | bytes 18874432 | tf_op jit(solution)/shard_map/jit(_take)/gather | solution.py:301
  300.0 9.5 %broadcast_select_fusion = f32[16,9,128,128]{3,2,1,0:T(8,128)} fusion(f32[16,9,128,128]{3,2,1,0:T(8,128)} %gather_fusion.5, pred[16]{0:T(512)(128)(4,1)S(1)} %compare_and_fusion.6), kind=kLoop, calls=%fused_computation.12 | loop fusion | flops 2359296 | bytes 18874384 | tf_op jit(solution)/shard_map/jit(_take)/select_n | solution.py:301
  309.5 10.1 %all-to-all-start.2 = ((f32[16,9,128,128]{3,2,1,0:T(8,128)}), f32[16,9,128,128]{3,2,1,0:T(8,128)}, u32[]{:S(2)}, u32[]{:S(2)}) async-start(f32[16,9,128,128]{3,2,1,0:T(8,128)} %broadcast_select_fusion), calls=%async_computation.2 | async-start | bytes 18874368 | tf_op jit(solution)/shard_map/all_to_all | solution.py:302
  321.9 50.7 %inverse_factor.3 = f32[1024,1024]{1,0:T(8,128)S(1)} custom-call(f32[1024,1024]{1,0:T(8,128)S(1)} %copy-done.5), custom_call_target="tpu_custom_call" | custom-call | flops 60000002048 | bytes 8388608 | tf_op jit(solution)/shard_map/inverse_factor/pallas_call | solution.py:125
  374.6 11.7 %fusion.41 = f32[640,1024]{1,0:T(8,128)S(1)} fusion(f32[640,1024]{1,0:T(8,128)} %bitcast.134, f32[1024,1024]{1,0:T(8,128)} %copy-done.6), kind=kOutput, calls=%fused_computation.134 | convolution fusion | flops 8053063680 | bytes 9437184 | tf_op jit(solution)/shard_map/dot_general | solution.py:178
  388.9 116.1 %all-to-all-done.2 = f32[16,9,128,128]{3,2,1,0:T(8,128)} async-done(((f32[16,9,128,128]{3,2,1,0:T(8,128)}), f32[16,9,128,128]{3,2,1,0:T(8,128)}, u32[]{:S(2)}, u32[]{:S(2)}) %all-to-all-start.2) | async-done | bytes 9437216 | tf_op jit(solution)/shard_map/all_to_all | solution.py:302
  505.0 6.0 gather_fusion.9
  511.0 6.2 gather_fusion.8
  525.2 52.5 %all-gather.12.cloned.1.call-done = f32[80,128,128]{2,1,0:T(8,128)} async-done(((f32[5,128,128]{2,1,0:T(8,128)}), f32[80,128,128]{2,1,0:T(8,128)}) %all-gather.12.cloned.1.call-update) | async-done | bytes 5242896 | tf_op jit(solution)/shard_map/all_gather | solution.py:295
  577.7 5.9 copy.80
  588.4 6.2 copy.81
  594.6 19.1 %fusion.42 = f32[1152,1024]{1,0:T(8,128)S(1)} fusion(f32[1152,1024]{1,0:T(8,128)} %bitcast.126, f32[1024,1024]{1,0:T(8,128)} %copy-done.6), kind=kOutput, calls=%fused_computation.135 | convolution fusion | flops 14495514624 | bytes 13631488 | tf_op jit(solution)/shard_map/dot_general | solution.py:178
  613.8 6.7 %fusion.5 = f32[640,1152]{1,0:T(8,128)S(1)} fusion(f32[1152,1024]{1,0:T(8,128)S(1)} %fusion.42, f32[80,8,9,128]{3,2,1,0:T(8,128)S(1)} %bitcast.122, f32[640,1024]{1,0:T(8,128)S(1)} %copy-done.12, pred[640]{0:T(1024)(128)(4,1)S(1)} %broadcast_compare_fusion.1, s32[640]{0:T(1024)S(1)} %add_bitcast_fusion), kind=kOutput, calls=%fused_computation.18 | convolution fusion | flops 4533288960 | bytes 13241472 | tf_op jit(solution)/shard_map/dot_general | solution.py:178
  (137 shorter events, 68.7 us)
Async XLA Ops:
  7.2 123.6 %all-gather.6.cloned.1.call-start = ((), (), s32[]{:S(2)}) async-start(), calls=%async_computation.3 | async-start | bytes 9437184 | tf_op jit(solution)/shard_map/all_gather | solution.py:220
  20.1 6.4 %copy-start.14 = (f32[5,1,128,10,1,128]{5,4,3,2,1,0:T(1,128)S(1)}, f32[5,1,128,10,1,128]{5,4,3,2,1,0:T(1,128)}, u32[]{:S(2)}) copy-start(f32[5,1,128,10,1,128]{5,4,3,2,1,0:T(1,128)} %param.13) | copy-start | bytes 9830404
  20.1 98.9 %all-to-all-start = ((f32[16,1024,128]{2,1,0:T(8,128)}), f32[16,1024,128]{2,1,0:T(8,128)}, u32[]{:S(2)}, u32[]{:S(2)}) async-start(f32[16,1024,128]{2,1,0:T(8,128)} %copy-done), calls=%async_computation | async-start | bytes 16777216 | tf_op jit(solution)/shard_map/all_to_all | solution.py:228
  25.7 209.4 %all-reduce.2.cloned.1.call-start = ((), (), s32[]{:S(2)}) async-start(), calls=%async_computation.5 | async-start | bytes 1048576 | tf_op jit(solution)/shard_map/psum | solution.py:266
  29.8 52.6 %copy-start.18 = (f32[1,8,1,128,1024]{4,3,2,1,0:T(8,128)S(1)}, f32[1,8,1,128,1024]{4,3,2,1,0:T(8,128)}, u32[]{:S(2)}) copy-start(f32[1,8,1,128,1024]{4,3,2,1,0:T(8,128)} %param.10) | copy-start | bytes 12582916
  137.5 3.7 copy-start.2
  141.2 7.4 %copy-start.13 = (f32[10,128,1024]{2,1,0:T(8,128)}, f32[10,128,1024]{2,1,0:T(8,128)S(1)}, u32[]{:S(2)}) copy-start(f32[10,128,1024]{2,1,0:T(8,128)S(1)} %broadcast_select_fusion.1) | copy-start | bytes 15728644
  141.2 4.5 copy-start.7
  145.7 89.6 %copy-start.19 = (s32[2,64]{1,0:T(2,128)S(1)}, s32[2,64]{1,0:T(2,128)}, u32[]{:S(2)}) copy-start(s32[2,64]{1,0:T(2,128)} %param.12) | copy-start | bytes 1540
  150.3 169.4 %all-gather.10.cloned.1.call-start = ((), (), s32[]{:S(2)}) async-start(), calls=%async_computation.6 | async-start | bytes 4718592 | tf_op jit(solution)/shard_map/all_gather | solution.py:267
  237.6 20.8 %all-to-all-start.1 = ((f32[16,128,128]{2,1,0:T(8,128)}), f32[16,128,128]{2,1,0:T(8,128)S(1)}, u32[]{:S(2)}, u32[]{:S(2)}) async-start(f32[16,128,128]{2,1,0:T(8,128)} %broadcast_select_fusion.3), calls=%async_computation.1 | async-start | bytes 2097152 | tf_op jit(solution)/shard_map/all_to_all | solution.py:288
  244.6 130.0 %all-gather.8.cloned.1.call-start = ((), (), s32[]{:S(2)}) async-start(), calls=%async_computation.4 | async-start | bytes 2949120 | tf_op jit(solution)/shard_map/all_gather | solution.py:292
  259.5 21.7 %slice-start = ((s8[5242880]{0:T(1024)(128)(4,1)}), s8[1048576]{0:T(1024)(128)(4,1)S(1)}, s32[]{:S(2)}) async-start(s8[5242880]{0:T(1024)(128)(4,1)} %bitcast.113), calls=%async_computation.8 | async-start | bytes 2097152
  261.5 316.1 %all-gather.12.cloned.1.call-start = ((), (), s32[]{:S(2)}) async-start(), calls=%async_computation.7 | async-start | bytes 5570560 | tf_op jit(solution)/shard_map/all_gather | solution.py:295
  261.7 18.9 %copy-start.16 = (f32[5,128,128]{2,1,0:T(8,128)S(1)}, f32[5,128,128]{2,1,0:T(8,128)}, u32[]{:S(2)}) copy-start(f32[5,128,128]{2,1,0:T(8,128)} %fusion.22) | copy-start | bytes 983044
  261.7 19.6 %slice-start.1 = ((s8[5242880]{0:T(1024)(128)(4,1)}), s8[4194304]{0:T(1024)(128)(4,1)S(1)}, s32[]{:S(2)}) async-start(s8[5242880]{0:T(1024)(128)(4,1)} %bitcast.113), calls=%async_computation.9 | async-start | bytes 8388608
  261.7 19.6 %copy-start.8 = (f32[1024,1024]{1,0:T(8,128)S(1)}, f32[1024,1024]{1,0:T(8,128)}, u32[]{:S(2)}) copy-start(f32[1024,1024]{1,0:T(8,128)} %fusion.40) | copy-start | bytes 12582916
  280.6 18.6 %collective-permute-start = (f32[5,128,128]{2,1,0:T(8,128)S(1)}, f32[5,128,128]{2,1,0:T(8,128)S(1)}, u32[]{:S(2)}, u32[]{:S(2)}) collective-permute-start(f32[5,128,128]{2,1,0:T(8,128)S(1)} %copy-done.16), channel_id=1, source_target_pairs={{0,0},{1,8},{2,16},{3,24},{4,32},{5,40},{6,48},{7,56},{8,1},{9,9},... | collective-permute-start | bytes 983048 | tf_op jit(solution)/shard_map/ppermute | solution.py:294
  309.5 195.6 %all-to-all-start.2 = ((f32[16,9,128,128]{3,2,1,0:T(8,128)}), f32[16,9,128,128]{3,2,1,0:T(8,128)}, u32[]{:S(2)}, u32[]{:S(2)}) async-start(f32[16,9,128,128]{3,2,1,0:T(8,128)} %broadcast_select_fusion), calls=%async_computation.2 | async-start | bytes 18874368 | tf_op jit(solution)/shard_map/all_to_all | solution.py:302
  511.0 6.2 copy-start.10
  588.4 25.3 %slice-start.2 = ((s8[5242880]{0:T(1024)(128)(4,1)}), s8[1048576]{0:T(1024)(128)(4,1)S(1)}, s32[]{:S(2)}) async-start(s8[5242880]{0:T(1024)(128)(4,1)} %bitcast.120), calls=%async_computation.10 | async-start | bytes 2097152
  594.6 19.2 %slice-start.3 = ((s8[5242880]{0:T(1024)(128)(4,1)}), s8[4194304]{0:T(1024)(128)(4,1)S(1)}, s32[]{:S(2)}) async-start(s8[5242880]{0:T(1024)(128)(4,1)} %bitcast.120), calls=%async_computation.11 | async-start | bytes 8388608
  594.6 19.2 %copy-start.12 = (f32[640,1024]{1,0:T(8,128)S(1)}, f32[640,1024]{1,0:T(8,128)}, u32[]{:S(2)}) copy-start(f32[640,1024]{1,0:T(8,128)} %copy-done.11) | copy-start | bytes 7864324
  613.8 6.7 %copy-start.15 = (f32[640,1,128]{2,1,0:T(1,128)S(1)}, f32[640,1,128]{2,1,0:T(1,128)}, u32[]{:S(2)}) copy-start(f32[640,1,128]{2,1,0:T(1,128)} %constant_dynamic-slice_fusion) | copy-start | bytes 983044
  (9 other events, 19.3 us)
Sparse Core Ops, SparseCore 0:
  12.8 108.8 all-gather.5
  150.4 84.6 all-reduce.1
  236.9 36.6 all-gather.9
  275.2 36.5 all-gather.7
  313.4 264.2 all-gather.11

commit v2 on v1

--- a/solution.py
+++ b/solution.py
@@ -5,7 +5,7 @@
 from jax import lax
 from jax.experimental import pallas as pl
 from jax.experimental.pallas import tpu as pltpu
-from jax.sharding import PartitionSpec as P
+from jax.sharding import Mesh, PartitionSpec as P
 
 PANEL = 1024
 BLOCK = 128
@@ -71,9 +71,19 @@
             block[stop:, :] = jnp.where(inside, 0.0, block[stop:, :]) - change
 
 
-def inverse_factor_kernel(matrix, state, block, scaled):
-    count = matrix.shape[0] // BLOCK
-    state[...] = matrix[...]
+def inverse_factor_kernel(source, state, block, scaled):
+    count = state.shape[0] // BLOCK
+    if len(source.shape) == 2:
+        state[...] = source[...]
+    else:
+        kept = source.shape[2]
+        for i in range(count):
+            for k in range(i, count):
+                if k - i < kept:
+                    part = source[k % 2, k // 2, k - i]
+                else:
+                    part = source[i % 2, i // 2, count + i - k].T
+                state[i * BLOCK : (i + 1) * BLOCK, k * BLOCK : (k + 1) * BLOCK] = part
     row_ids = lax.broadcasted_iota(jnp.int32, (BLOCK, BLOCK), 0)
     col_ids = lax.broadcasted_iota(jnp.int32, (BLOCK, BLOCK), 1)
 
@@ -119,8 +129,7 @@
     lax.fori_loop(0, count, clear, 0)
 
 
-def inverse_factor(matrix):
-    order = matrix.shape[0]
+def inverse_factor(source, order):
     whole = pl.BlockSpec(memory_space=pltpu.VMEM)
     return pl.pallas_call(
         inverse_factor_kernel,
@@ -133,7 +142,7 @@
             flops=60_000_000_000, bytes_accessed=8 * order * order, transcendentals=0
         ),
         name="inverse_factor",
-    )(matrix)
+    )(source)
 
 
 def spread_kernel(slots, source, target):
@@ -162,11 +171,106 @@
     )(slots, source)
 
 
-def ranks(targets):
+def copy_kernel(slots, source, target):
+    target[...] = source[...]
+
+
+def pick_blocks(slots, source):
+    shape = (slots.shape[0],) + source.shape[1:]
+    block = (1,) + source.shape[1:]
+    return pl.pallas_call(
+        copy_kernel,
+        out_shape=jax.ShapeDtypeStruct(shape, F32),
+        grid_spec=pltpu.PrefetchScalarGridSpec(
+            num_scalar_prefetch=1,
+            grid=(shape[0],),
+            in_specs=[pl.BlockSpec(block, lambda i, s: (s[i], 0, 0))],
+            out_specs=pl.BlockSpec(block, lambda i, s: (i, 0, 0)),
+        ),
+        cost_estimate=pl.CostEstimate(
+            flops=0, bytes_accessed=8 * shape[0] * shape[1] * shape[2], transcendentals=0
+        ),
+        name="pick_blocks",
+    )(slots, source)
+
+
+def place_kernel(slots, there, dests, update, product, target):
+    k = pl.program_id(0)
+    for b in range(update.shape[1] // BLOCK):
+        rows = slice(b * BLOCK, (b + 1) * BLOCK)
+        change = update[0, rows, :] - product[rows, :]
+        target[dests[b], 0] = jnp.where(there[k] > 0, change, 0.0)
+
+
+def place_updates(slots, there, dests, updates, product, groups):
+    count, rows = slots.shape[0], updates.shape[1]
+    return pl.pallas_call(
+        place_kernel,
+        out_shape=jax.ShapeDtypeStruct((groups, count, BLOCK, BLOCK), F32),
+        grid_spec=pltpu.PrefetchScalarGridSpec(
+            num_scalar_prefetch=3,
+            grid=(count,),
+            in_specs=[
+                pl.BlockSpec((1, rows, BLOCK), lambda k, s, t, d: (s[k], 0, 0)),
+                pl.BlockSpec((rows, BLOCK), lambda k, s, t, d: (0, k)),
+            ],
+            out_specs=pl.BlockSpec(
+                (groups, 1, BLOCK, BLOCK), lambda k, s, t, d: (0, k, 0, 0)
+            ),
+        ),
+        cost_estimate=pl.CostEstimate(
+            flops=0,
+            bytes_accessed=4 * BLOCK * count * (2 * rows + groups * BLOCK),
+            transcendentals=0,
+        ),
+        name="place_updates",
+    )(slots, there, dests, updates, product)
+
+
+def finish_kernel(slots, there, top, root, panel, first, second, product, target):
+    i = pl.program_id(0)
+    columns = first.shape[1] + 1
+    target[pl.ds(0, BLOCK, stride=columns), :] = panel[...]
+    for k in range(1, columns):
+        here = pl.ds(k, BLOCK, stride=columns)
+        total = root[here, :]
+        total = total + jnp.where(there[0, i] > 0, first[0, k - 1], 0.0)
+        total = total + jnp.where(there[1, i] > 0, second[0, k - 1], 0.0)
+        total = total - product[:, (k - 1) * BLOCK : k * BLOCK]
+        target[here, :] = jnp.where(top[i] > 0, 0.0, total)
+
+
+def finish(slots, there, top, root, panel, received, product):
+    columns = received.shape[1] + 1
+    root_rows = slots.shape[1]
+    rows = BLOCK * columns
+    block = (1,) + received.shape[1:]
+    return pl.pallas_call(
+        finish_kernel,
+        out_shape=jax.ShapeDtypeStruct(root.shape, F32),
+        grid_spec=pltpu.PrefetchScalarGridSpec(
+            num_scalar_prefetch=3,
+            grid=(root_rows,),
+            in_specs=[
+                pl.BlockSpec((rows, BLOCK), lambda i, s, t, p: (i, 0)),
+                pl.BlockSpec((BLOCK, BLOCK), lambda i, s, t, p: (i, 0)),
+                pl.BlockSpec(block, lambda i, s, t, p: (s[0, i], 0, 0, 0)),
+                pl.BlockSpec(block, lambda i, s, t, p: (s[1, i], 0, 0, 0)),
+                pl.BlockSpec((BLOCK, product.shape[1]), lambda i, s, t, p: (i, 0)),
+            ],
+            out_specs=pl.BlockSpec((rows, BLOCK), lambda i, s, t, p: (i, 0)),
+        ),
+        cost_estimate=pl.CostEstimate(
+            flops=0, bytes_accessed=4 * BLOCK * 5 * rows * root_rows, transcendentals=0
+        ),
+        name="finish",
+    )(slots, there, top, root, panel, received, received, product)
+
+
+def ranks(targets, keys):
     same = targets[..., :, None] == targets[..., None, :]
-    length = targets.shape[-1]
-    earlier = jnp.arange(length)[:, None] > jnp.arange(length)[None, :]
-    return jnp.sum(jnp.logical_and(same, earlier).astype(jnp.int32), axis=-1)
+    before = keys[..., None, :] < keys[..., :, None]
+    return jnp.sum(jnp.logical_and(same, before).astype(jnp.int32), axis=-1)
 
 
 def locate(matches, values):
@@ -180,20 +284,45 @@
     )
 
 
+def exchange(values, axes):
+    return lax.all_to_all(values, axes, split_axis=0, concat_axis=0, tiled=True)
+
+
+def shift(values, axis, size, step):
+    return lax.ppermute(values, axis, [(i, (i + step) % size) for i in range(size)])
+
+
+def ring(values, axis, size):
+    return [values] + [shift(values, axis, size, d) for d in range(1, size)]
+
+
+def in_order(pieces, axis):
+    size = len(pieces)
+    return jnp.take(
+        jnp.stack(pieces), (lax.axis_index(axis) - jnp.arange(size, dtype=jnp.int32)) % size, axis=0
+    )
+
+
+def after(values, *earlier):
+    return lax.optimization_barrier((values,) + earlier)[0]
+
+
 def per_device(child_pivot, child_border, child_update, index_map, root_front):
-    n_rows = lax.axis_size("row")
-    n_cols = lax.axis_size("col")
+    row, col = ("x", "z_hi"), ("y", "core")
+    joined = ("half",) + row
+    n_rows = lax.axis_size("x") * lax.axis_size("z_hi")
+    n_y, n_core = lax.axis_size("y"), lax.axis_size("core")
+    n_cols = n_y * n_core
     groups = 2 * n_rows
     sibling = lax.axis_index("half")
-    row_index = lax.axis_index("row")
-    col_index = lax.axis_index("col")
+    row_index = lax.axis_index(row)
+    col_index = lax.axis_index(col)
     group = sibling * n_rows + row_index
     block_count = child_border.shape[1]
     pivots = child_border.shape[4]
     local_rows = block_count * BLOCK
     root_rows = root_front.shape[0]
     root_cols = root_front.shape[3]
-    capacity = 2
     numbers = jnp.arange(block_count, dtype=jnp.int32)
 
     child_map = lax.dynamic_index_in_dim(index_map, sibling, 0, keepdims=False).reshape(
@@ -201,7 +330,9 @@
     )
     by_class = child_map.T
     class_dest = by_class % n_cols
-    class_rank = ranks(class_dest)
+    class_rank = ranks(
+        class_dest, jnp.where(by_class < n_cols, 0, block_count) + numbers[None, :]
+    )
     col_dest = lax.dynamic_index_in_dim(class_dest, col_index, 0, keepdims=False)
     col_rank = lax.dynamic_index_in_dim(class_rank, col_index, 0, keepdims=False)
     row_map = lax.dynamic_index_in_dim(by_class, row_index, 0, keepdims=False)
@@ -209,62 +340,42 @@
     row_rank = lax.dynamic_index_in_dim(class_rank, row_index, 0, keepdims=False)
 
     border = child_border.reshape(block_count, BLOCK, pivots)
+
     wanted, _ = locate(
         jnp.logical_and(
             row_dest[None, :] == col_index,
-            row_rank[None, :] == jnp.arange(capacity, dtype=jnp.int32)[:, None],
+            row_rank[None, :] == jnp.arange(2, dtype=jnp.int32)[:, None],
         ),
         numbers,
     )
-    own_wanted = jnp.take(border, wanted, axis=0)
-    every_wanted = lax.all_gather(own_wanted, "row", axis=0, tiled=True)
-
-    sending = spread_columns(
-        col_dest * capacity + col_rank,
-        child_update.reshape(local_rows * block_count, BLOCK),
-        n_cols * capacity,
-        block_count,
-    )
-    arrived = lax.all_to_all(sending, "col", split_axis=0, concat_axis=0, tiled=True)
-
-    flat_source = numbers[:, None] * capacity + class_rank
+    borders = lax.all_gather(pick_blocks(wanted, border), row, axis=0, tiled=True)
+    updates = exchange(
+        spread_columns(
+            col_dest * 2 + col_rank,
+            child_update.reshape(local_rows * block_count, BLOCK),
+            2 * n_cols,
+            block_count,
+        ),
+        col,
+    )
+
+    flat_source = numbers[:, None] * 2 + class_rank
     wanted_roots = jnp.arange(root_cols, dtype=jnp.int32) * n_cols + col_index
     source_slots, source_there = locate(
         by_class.reshape(1, -1) == wanted_roots[:, None], flat_source.reshape(-1)
     )
 
-    inverse = inverse_factor(child_pivot[0])
+    inverse = inverse_factor(child_pivot[0], pivots)
     own_factor = times_transposed(border.reshape(local_rows, pivots), inverse, exact)
-    column_border = jnp.take(every_wanted, source_slots, axis=0)
-    column_update = jnp.take(arrived, source_slots, axis=0)
-
-    def schur(first, last):
-        count = last - first
-        factor = times_transposed(
-            column_border[first:last].reshape(count * BLOCK, pivots), inverse, exact
-        )
-        product = lax.dot_general(
-            factor.reshape(count, BLOCK, pivots),
-            own_factor,
-            (((2,), (1,)), ((), ())),
-            precision=close,
-            preferred_element_type=F32,
-        )
-        product = jnp.transpose(product, (0, 2, 1))
-        there = source_there[first:last, None, None]
-        return jnp.where(there, column_update[first:last] - product, 0.0).reshape(
-            count, block_count, BLOCK, BLOCK
-        )
-
-    panel_update = schur(0, 1)[0]
+
     root_view = root_front.reshape(root_rows, BLOCK, root_cols, BLOCK)
-
-    top_index, top_there = locate(row_map[None, :] == numbers[:, None], numbers)
-    top_part = jnp.where(top_there[:, None, None], jnp.take(panel_update, top_index, axis=0), 0.0)
-    is_owner = jnp.logical_and(sibling == 0, row_index == numbers)
-    top_part = top_part + jnp.where(is_owner[:, None, None], root_view[0, :, 0, :][None], 0.0)
-    leading_cols = lax.psum(top_part, ("half", "row")).reshape(PANEL, BLOCK)
-    leading = lax.all_gather(leading_cols, "col", axis=1, tiled=True)
+    panel_slot = source_slots[0]
+    panel_border = lax.dynamic_index_in_dim(borders, panel_slot, 0, keepdims=False)
+    panel_factor = times_transposed(panel_border, inverse, exact)
+    panel_update = lax.dynamic_index_in_dim(
+        updates, panel_slot, 0, keepdims=False
+    ) - times_transposed(own_factor, panel_factor, close)
+    panel_update = jnp.where(source_there[0], panel_update, 0.0).reshape(block_count, BLOCK, BLOCK)
 
     sent_blocks, _ = locate(
         (row_map % groups)[None, :] == jnp.arange(groups, dtype=jnp.int32)[:, None], numbers
@@ -284,24 +395,46 @@
             base = base + jnp.where(got_there[half].reshape(shape), picked, 0.0)
         return base
 
-    panel_sent = jnp.take(panel_update, sent_blocks, axis=0)
-    panel_got = lax.all_to_all(
-        panel_sent, ("half", "row"), split_axis=0, concat_axis=0, tiled=True
-    )
+    panel_got = exchange(jnp.take(panel_update, sent_blocks, axis=0), joined)
     own_panel = extend_add(root_view[:, :, 0, :], panel_got)
-    panel_rows = lax.all_gather(own_panel, "col", axis=2, tiled=True)
+
+    n_x, n_z = lax.axis_size("x"), lax.axis_size("z_hi")
+    corner = jnp.where(sibling == 0, own_panel[0], shift(own_panel[0], "half", 2, 1))
+    corner = in_order(ring(corner, "z_hi", n_z), "z_hi")
+    leading_column = in_order(ring(corner, "x", n_x), "x").reshape(n_rows, BLOCK, BLOCK)
+    kept = n_cols // 2 + 1
+    kept_rows = (col_index - jnp.arange(kept, dtype=jnp.int32)) % n_cols
+    kept_blocks = jnp.take(leading_column, kept_rows, axis=0)
+    leading = in_order(ring(kept_blocks, "y", n_y), "y")
+    other_core = shift(leading, "core", 2, 1)
+    is_first = lax.axis_index("core") == 0
+    leading = jnp.stack(
+        [jnp.where(is_first, leading, other_core), jnp.where(is_first, other_core, leading)]
+    )
+
+    panel_rows = lax.all_gather(after(own_panel, leading), col, axis=2, tiled=True)
     swaps = [(r * n_cols + c, c * n_rows + r) for r in range(n_rows) for c in range(n_cols)]
-    swapped = lax.ppermute(own_panel, ("row", "col"), swaps)
-    column_panel = lax.all_gather(swapped, ("half", "row"), axis=0, tiled=False).reshape(
-        2, n_rows, root_rows, BLOCK, BLOCK
-    )
-    column_panel = jnp.transpose(column_panel, (2, 0, 3, 1, 4)).reshape(root_cols, BLOCK, PANEL)
-
-    rest_update = schur(1, root_cols)
-    rest_sent = jnp.take(jnp.transpose(rest_update, (1, 0, 2, 3)), sent_blocks, axis=0)
-    rest_got = lax.all_to_all(rest_sent, ("half", "row"), split_axis=0, concat_axis=0, tiled=True)
-
-    root_inverse = inverse_factor(leading)
+    swapped = lax.ppermute(after(own_panel, leading), row + col, swaps)
+    by_z = in_order(ring(in_order(ring(swapped, "half", 2), "half"), "z_hi", n_z), "z_hi")
+    column_panel = in_order(ring(by_z, "x", n_x), "x")
+    column_panel = jnp.transpose(column_panel, (3, 2, 4, 0, 1, 5)).reshape(
+        root_cols, BLOCK, PANEL
+    )
+
+    rest_factor = times_transposed(
+        pick_blocks(source_slots[1:], borders).reshape(-1, pivots), inverse, exact
+    )
+    rest_sent = place_updates(
+        source_slots[1:],
+        source_there[1:].astype(jnp.int32),
+        row_map % groups,
+        updates,
+        times_transposed(own_factor, rest_factor, close),
+        groups,
+    )
+    rest_got = exchange(after(rest_sent, panel_got), joined)
+
+    root_inverse = inverse_factor(leading, PANEL)
     factor_rows = times_transposed(panel_rows.reshape(root_rows * BLOCK, PANEL), root_inverse, exact)
     column_factor = times_transposed(
         column_panel[1:].reshape((root_cols - 1) * BLOCK, PANEL), root_inverse, exact
@@ -314,31 +447,35 @@
         is_top[:, None], jnp.arange(PANEL, dtype=jnp.int32)[None, :] > global_rows[:, None]
     )
     factor_rows = jnp.where(above, 0.0, factor_rows)
-    rest = jnp.transpose(root_view[:, :, 1:, :], (0, 2, 1, 3))
-    rest = extend_add(rest, rest_got)
-    trailing = jnp.transpose(rest, (0, 2, 1, 3)).reshape(
-        root_rows * BLOCK, -1
-    ) - times_transposed(factor_rows, column_factor, close)
     panel_part = lax.dynamic_index_in_dim(
         factor_rows.reshape(-1, n_cols, BLOCK), col_index, 1, keepdims=False
     )
-    remainder = jnp.where(is_top[:, None], 0.0, trailing)
-    combined = jnp.concatenate([panel_part, remainder], axis=1)
+    combined = finish(
+        got_slots,
+        got_there.astype(jnp.int32),
+        (my_roots < n_cols).astype(jnp.int32),
+        root_front.reshape(root_rows * BLOCK * root_cols, BLOCK),
+        panel_part,
+        rest_got,
+        times_transposed(factor_rows, column_factor, close),
+    )
     return (own_factor.reshape(child_border.shape), combined.reshape(root_front.shape))
 
 
 def solution(mesh):
+    fine = Mesh(mesh.devices.reshape(2, 4, 2, 4, 2), ("half", "x", "z_hi", "y", "core"))
+    row, col = ("x", "z_hi"), ("y", "core")
     in_specs = (
         P("half", None, None),
-        P("half", None, "row", None, None),
-        P("half", None, "row", None, None, "col", None),
+        P("half", None, row, None, None),
+        P("half", None, row, None, None, col, None),
         P(),
-        P(None, ("half", "row"), None, None, "col", None),
+        P(None, ("half",) + row, None, None, col, None),
     )
     out_specs = (
-        P("half", None, "row", None, None),
-        P(None, ("half", "row"), None, None, "col", None),
+        P("half", None, row, None, None),
+        P(None, ("half",) + row, None, None, col, None),
     )
     return jax.shard_map(
-        per_device, mesh=mesh, in_specs=in_specs, out_specs=out_specs, check_vma=False
-    )
+        per_device, mesh=fine, in_specs=in_specs, out_specs=out_specs, check_vma=False
+    )

time: 642 us -> 589 us (0.917)
  the two profiles are of different devices: /device:TPU:42 before, /device:TPU:6 now
where the time goes in v2:
time: 589 us; the launch traced here: 578 us
  waiting for transfers between devices  216 us (37%)
  Pallas kernels  133 us (23%)
  matrix products  98.3 us (17%)
  local copies, waits for them, and re-layouts  50.9 us (9%)
  starting transfers between devices  39.3 us (7%)
  other arithmetic  23.9 us (4%)
  between operations  15.3 us (3%)
    ppermute x14, waiting for transfers between devices, shift(): lax.ppermute(values, axis, [(i, (i + step) % size) for i in range(size)])  168 us
    pallas_call x2, Pallas kernels, inverse_factor(): pl.pallas_call(inverse_factor_kernel, out_shape=jax.ShapeDtypeStruct((ord...  102 us
    dot_general x8, matrix products, times_transposed(): lax.dot_general(left, right, (((1,), (1,)), ((), ())), precision=precisio...  98.3 us
    all_gather x1, waiting for transfers between devices, per_device(): lax.all_gather(pick_blocks(wanted, border), row, axis=0, tiled=True)  22.7 us
    ppermute x14, starting transfers between devices, shift(): lax.ppermute(values, axis, [(i, (i + step) % size) for i in range(size)])  19.1 us
    all_to_all x3, waiting for transfers between devices, exchange(): return lax.all_to_all(values, axes, split_axis=0, concat_axis=0, tiled=True)  16.4 us
    all_to_all x3, starting transfers between devices, exchange(): return lax.all_to_all(values, axes, split_axis=0, concat_axis=0, tiled=True)  15.8 us
    unnamed x30, local copies, waits for them, and re-layouts  15.8 us
  transfers between devices with their start and end apart: 20, of which 15 were waited for; matrix products, arithmetic and copies ran while one was open for 25% of the time, Pallas kernels for 21%

profile of v2, /device:TPU:6, one launch (start us, length us, event | category | flops | bytes accessed | tf_op | source)
XLA Modules:
  0.0 577.5 jit_solution(4698078324893591599)
XLA Ops:
  19.4 5.2 all-to-all-start
  31.3 50.7 %inverse_factor.2 = f32[1024,1024]{1,0:T(8,128)S(1)} custom-call(f32[1024,1024]{1,0:T(8,128)S(1)} %bitcast.118), custom_call_target="tpu_custom_call" | custom-call | flops 60000002048 | bytes 8388608 | tf_op jit(solution)/shard_map/inverse_factor/pallas_call | solution.py:134
  84.1 14.9 %fusion.45 = f32[1024,1024]{1,0:T(8,128)} fusion(f32[1024,1024]{1,0:T(8,128)S(1)} %bitcast.126, f32[1024,1024]{1,0:T(8,128)S(1)} %inverse_factor.2), kind=kOutput, calls=%fused_computation.184 | convolution fusion | flops 12884901888 | bytes 12582912 | tf_op jit(solution)/shard_map/dot_general | solution.py:282
  99.0 22.7 %all-gather.3.cloned.1.call-done.source = f32[16,128,1024]{2,1,0:T(8,128)} async-done(((f32[2,128,1024]{2,1,0:T(8,128)}), f32[16,128,1024]{2,1,0:T(8,128)}) %all-gather.3.cloned.1.call-update) | async-done | bytes 8388624 | tf_op jit(solution)/shard_map/all_gather | solution.py:351
  121.7 6.7 %fusion.9 = f32[128,1024]{1,0:T(8,128)S(1)} fusion(f32[1024,1024]{1,0:T(8,128)} %copy-done.2, f32[16,128,1024]{2,1,0:T(8,128)} %all-gather.3.cloned.1.call-done.source, s32[]{:T(128)S(6)} %select_n.361), kind=kOutput, calls=%fused_computation.35 | convolution fusion | flops 1610612736 | bytes 5242884 | tf_op jit(solution)/shard_map/dot_general | solution.py:282
  134.4 5.9 %all-to-all-start.1 = ((f32[16,128,128]{2,1,0:T(8,128)}), f32[16,128,128]{2,1,0:T(8,128)S(1)}, u32[]{:S(2)}, u32[]{:S(2)}) async-start(f32[16,128,128]{2,1,0:T(8,128)} %broadcast_select_fusion.2), calls=%async_computation.1 | async-start | bytes 2097152 | tf_op jit(solution)/shard_map/all_to_all | solution.py:288
  140.9 16.4 %all-to-all-done.1 = f32[16,128,128]{2,1,0:T(8,128)S(1)} async-done(((f32[16,128,128]{2,1,0:T(8,128)}), f32[16,128,128]{2,1,0:T(8,128)S(1)}, u32[]{:S(2)}, u32[]{:S(2)}) %all-to-all-start.1) | async-done | bytes 1048608 | tf_op jit(solution)/shard_map/all_to_all | solution.py:288
  184.7 7.7 %collective-permute-done.7 = f32[5,128,128]{2,1,0:T(8,128)S(1)} collective-permute-done((f32[5,128,128]{2,1,0:T(8,128)S(1)}, f32[5,128,128]{2,1,0:T(8,128)S(1)}, u32[]{:S(2)}, u32[]{:S(2)}) %collective-permute-start.7) | collective-permute-done | bytes 327712 | tf_op jit(solution)/shard_map/ppermute | solution.py:292
  207.1 8.0 %pick_blocks.3 = f32[9,128,1024]{2,1,0:T(8,128)} custom-call(s32[9]{0:T(128)} %slice.43.slots, f32[16,128,1024]{2,1,0:T(8,128)} %all-gather.3.cloned.1.call-done.source), custom_call_target="tpu_custom_call" | custom-call | bytes 9437184 | tf_op jit(solution)/shard_map/pick_blocks/pallas_call | solution.py:181
  215.1 8.5 %collective-permute-done.9 = f32[5,128,128]{2,1,0:T(8,128)S(1)} collective-permute-done((f32[5,128,128]{2,1,0:T(8,128)S(1)}, f32[5,128,128]{2,1,0:T(8,128)S(1)}, u32[]{:S(2)}, u32[]{:S(2)}) %collective-permute-start.9) | collective-permute-done | bytes 327712 | tf_op jit(solution)/shard_map/ppermute | solution.py:417
  224.7 20.2 %fusion.47 = f32[1152,1024]{1,0:T(8,128)} fusion(f32[1152,1024]{1,0:T(8,128)} %bitcast.122, f32[1024,1024]{1,0:T(8,128)} %copy-done.2), kind=kOutput, calls=%fused_computation.186 | convolution fusion | flops 14495514624 | bytes 13631488 | tf_op jit(solution)/shard_map/dot_general | solution.py:282
  251.9 13.3 %fusion.48.product = f32[1024,1152]{1,0:T(8,128)} fusion(f32[1024,1024]{1,0:T(8,128)} %fusion.45, f32[1152,1024]{1,0:T(8,128)} %fusion.47), kind=kOutput, calls=%fused_computation.187 | convolution fusion | flops 7247757312 | bytes 13631488 | tf_op jit(solution)/shard_map/dot_general | solution.py:282
  265.2 10.8 %place_updates.1 = f32[16,9,128,128]{3,2,1,0:T(8,128)} custom-call(s32[9]{0:T(128)} %slice.43.slots, s32[9]{0:T(128)} %slice_convert_fusion.there, s32[8]{0:T(128)} %copy-done.13, f32[16,1024,128]{2,1,0:T(8,128)} %all-to-all-done.update, f32[1024,1152]{1,0:T(8,128)} %fusion.48.product), custom_call_target="tpu_custom_call" | custom-call | bytes 18874368 | tf_op jit(solution)/shard_map/place_updates/pallas_call | solution.py:207
  292.4 50.9 %inverse_factor.3 = f32[1024,1024]{1,0:T(8,128)S(1)} custom-call(f32[2,4,5,128,128]{4,3,2,1,0:T(8,128)S(1)} %pad_maximum_fusion.1.source), custom_call_target="tpu_custom_call" | custom-call | flops 60000002048 | bytes 8388608 | tf_op jit(solution)/shard_map/inverse_factor/pallas_call | solution.py:134
  345.4 114.7 %collective-permute-done.14 = f32[2,2,5,128,128]{4,3,2,1,0:T(8,128)S(1)} collective-permute-done((f32[2,2,5,128,128]{4,3,2,1,0:T(8,128)S(1)}, f32[2,2,5,128,128]{4,3,2,1,0:T(8,128)S(1)}, u32[]{:S(2)}, u32[]{:S(2)}) %collective-permute-start.14) | collective-permute-done | bytes 1310752 | tf_op jit(solution)/shard_map/ppermute | solution.py:292
  460.2 25.8 %collective-permute-done.13 = f32[2,2,5,128,128]{4,3,2,1,0:T(8,128)S(1)} collective-permute-done((f32[2,2,5,128,128]{4,3,2,1,0:T(8,128)S(1)}, f32[2,2,5,128,128]{4,3,2,1,0:T(8,128)S(1)}, u32[]{:S(2)}, u32[]{:S(2)}) %collective-permute-start.13) | collective-permute-done | bytes 1310752 | tf_op jit(solution)/shard_map/ppermute | solution.py:292
  491.6 5.7 gather_fusion.7
  497.3 5.7 select_bitcast_fusion
  503.1 5.9 %copy.64 = f32[5,2,128,4,2,128]{2,5,4,3,1,0:T(8,128)} copy(f32[5,2,128,4,2,128]{5,2,0,1,4,3:T(8,128)} %select_bitcast_fusion) | data formatting | bytes 10485760 | tf_op jit(solution)/shard_map/jit(_take)/select_n | solution.py:301
  513.8 6.0 %copy.65 = f32[9,128,1024]{2,1,0:T(8,128)} copy(f32[9,128,1024]{1,2,0:T(8,128)} %slice.68) | data formatting | bytes 9437184 | tf_op jit(solution)/shard_map/slice | solution.py:440
  519.9 20.0 %fusion.49 = f32[1152,1024]{1,0:T(8,128)} fusion(f32[1152,1024]{1,0:T(8,128)} %bitcast.123, f32[1024,1024]{1,0:T(8,128)} %copy-done.4), kind=kOutput, calls=%fused_computation.188 | convolution fusion | flops 14495514624 | bytes 13631488 | tf_op jit(solution)/shard_map/dot_general | solution.py:282
  539.9 11.7 %fusion.46 = f32[640,1024]{1,0:T(8,128)S(1)} fusion(f32[640,1024]{1,0:T(8,128)} %bitcast.149, f32[1024,1024]{1,0:T(8,128)} %copy-done.4), kind=kOutput, calls=%fused_computation.185 | convolution fusion | flops 8053063680 | bytes 9437184 | tf_op jit(solution)/shard_map/dot_general | solution.py:282
  554.6 7.3 %fusion.2.product = f32[640,1152]{1,0:T(8,128)} fusion(f32[1152,1024]{1,0:T(8,128)S(1)} %copy-done.7, f32[640,1024]{1,0:T(8,128)S(1)} %fusion.46, s32[640]{0:T(1024)S(1)} %add_bitcast_fusion, pred[640]{0:T(1024)(128)(4,1)S(1)} %broadcast_compare_fusion), kind=kOutput, calls=%fused_computation.17 | convolution fusion | flops 4531814400 | bytes 10292352 | tf_op jit(solution)/shard_map/dot_general | solution.py:282
  562.0 8.2 %finish.1 = f32[6400,128]{1,0:T(8,128)} custom-call(s32[2,5]{1,0:T(2,128)} %copy.66.slots, s32[2,5]{1,0:T(2,128)} %get-tuple-element.25.there, s32[5]{0:T(128)} %compare_convert_fusion.2.top, f32[6400,128]{1,0:T(8,128)} %bitcast.120, f32[640,128]{1,0:T(8,128)} %bitcast.130, f32[16,9,128,128]{3,2,1,0:T(8,128)} %all-to-all-done.2.first.second, ...), custom_call_target="tpu_custom_call" | custom-call | bytes 16384000 | tf_op jit(solution)/shard_map/finish/pallas_call | solution.py:248
  (158 shorter events, 109.3 us)
Async XLA Ops:
  7.2 114.5 %all-gather.3.cloned.1.call-start = ((), (), s32[]{:S(2)}) async-start(), calls=%async_computation.3 | async-start | bytes 9437184 | tf_op jit(solution)/shard_map/all_gather | solution.py:351
  19.4 7.4 %copy-start.5 = (f32[5,1,128,10,1,128]{5,4,3,2,1,0:T(1,128)S(1)}, f32[5,1,128,10,1,128]{5,4,3,2,1,0:T(1,128)}, u32[]{:S(2)}) copy-start(f32[5,1,128,10,1,128]{5,4,3,2,1,0:T(1,128)} %param.11) | copy-start | bytes 9830404
  19.4 109.0 %all-to-all-start = ((f32[16,1024,128]{2,1,0:T(8,128)}), f32[16,1024,128]{2,1,0:T(8,128)}, u32[]{:S(2)}, u32[]{:S(2)}) async-start(f32[16,1024,128]{2,1,0:T(8,128)} %copy-done), calls=%async_computation | async-start | bytes 16777216 | tf_op jit(solution)/shard_map/all_to_all | solution.py:288
  31.3 52.8 %copy-start.8 = (f32[1,8,1,128,1024]{4,3,2,1,0:T(8,128)S(1)}, f32[1,8,1,128,1024]{4,3,2,1,0:T(8,128)}, u32[]{:S(2)}) copy-start(f32[1,8,1,128,1024]{4,3,2,1,0:T(8,128)} %param.8) | copy-start | bytes 12582916
  134.4 22.9 %all-to-all-start.1 = ((f32[16,128,128]{2,1,0:T(8,128)}), f32[16,128,128]{2,1,0:T(8,128)S(1)}, u32[]{:S(2)}, u32[]{:S(2)}) async-start(f32[16,128,128]{2,1,0:T(8,128)} %broadcast_select_fusion.2), calls=%async_computation.1 | async-start | bytes 2097152 | tf_op jit(solution)/shard_map/all_to_all | solution.py:288
  159.6 42.5 %copy-start.9 = (f32[5,128,128]{2,1,0:T(8,128)}, f32[5,128,128]{2,1,0:T(8,128)S(1)}, u32[]{:S(2)}) copy-start(f32[5,128,128]{2,1,0:T(8,128)S(1)} %fusion.13) | copy-start | bytes 983044
  159.6 4.3 collective-permute-start
  164.0 5.8 %collective-permute-start.1 = (f32[128,128]{1,0:T(8,128)S(1)}, f32[128,128]{1,0:T(8,128)S(1)}, u32[]{:S(2)}, u32[]{:S(2)}) collective-permute-start(f32[128,128]{1,0:T(8,128)S(1)} %broadcast_select_fusion.6), channel_id=1, source_target_pairs={{0,8},{8,0},{1,9},{9,1},{2,10},{10,2},{3,11},{11,3},{4,12},{12,4},... | collective-permute-start | bytes 196616 | tf_op jit(solution)/shard_map/ppermute | solution.py:292
  170.5 6.2 %collective-permute-start.4 = (f32[2,128,128]{2,1,0:T(8,128)S(1)}, f32[2,128,128]{2,1,0:T(8,128)S(1)}, u32[]{:S(2)}, u32[]{:S(2)}) collective-permute-start(f32[2,128,128]{2,1,0:T(8,128)S(1)} %broadcast_select_fusion.5), channel_id=1, source_target_pairs={{0,48},{16,0},{32,16},{48,32},{1,49},{17,1},{33,17},{49,33},{2,50}... | collective-permute-start | bytes 393224 | tf_op jit(solution)/shard_map/ppermute | solution.py:292
  172.0 6.5 %collective-permute-start.3 = (f32[2,128,128]{2,1,0:T(8,128)S(1)}, f32[2,128,128]{2,1,0:T(8,128)S(1)}, u32[]{:S(2)}, u32[]{:S(2)}) collective-permute-start(f32[2,128,128]{2,1,0:T(8,128)S(1)} %broadcast_select_fusion.5), channel_id=1, source_target_pairs={{0,32},{16,48},{32,0},{48,16},{1,33},{17,49},{33,1},{49,17},{2,34}... | collective-permute-start | bytes 393224 | tf_op jit(solution)/shard_map/ppermute | solution.py:292
  173.9 5.1 collective-permute-start.2
  180.4 11.9 %collective-permute-start.7 = (f32[5,128,128]{2,1,0:T(8,128)S(1)}, f32[5,128,128]{2,1,0:T(8,128)S(1)}, u32[]{:S(2)}, u32[]{:S(2)}) collective-permute-start(f32[5,128,128]{2,1,0:T(8,128)S(1)} %broadcast_select_fusion.4), channel_id=1, source_target_pairs={{0,6},{2,0},{4,2},{6,4},{1,7},{3,1},{5,3},{7,5},{8,14},{10,8},{12,... | collective-permute-start | bytes 983048 | tf_op jit(solution)/shard_map/ppermute | solution.py:292
  182.9 9.8 %collective-permute-start.6 = (f32[5,128,128]{2,1,0:T(8,128)S(1)}, f32[5,128,128]{2,1,0:T(8,128)S(1)}, u32[]{:S(2)}, u32[]{:S(2)}) collective-permute-start(f32[5,128,128]{2,1,0:T(8,128)S(1)} %broadcast_select_fusion.4), channel_id=1, source_target_pairs={{0,4},{2,6},{4,0},{6,2},{1,5},{3,7},{5,1},{7,3},{8,12},{10,14},{12... | collective-permute-start | bytes 983048 | tf_op jit(solution)/shard_map/ppermute | solution.py:292
  183.7 12.3 %collective-permute-start.5 = (f32[5,128,128]{2,1,0:T(8,128)S(1)}, f32[5,128,128]{2,1,0:T(8,128)S(1)}, u32[]{:S(2)}, u32[]{:S(2)}) collective-permute-start(f32[5,128,128]{2,1,0:T(8,128)S(1)} %broadcast_select_fusion.4), channel_id=1, source_target_pairs={{0,2},{2,4},{4,6},{6,0},{1,3},{3,5},{5,7},{7,1},{8,10},{10,12},{12... | collective-permute-start | bytes 983048 | tf_op jit(solution)/shard_map/ppermute | solution.py:292
  197.0 3.2 collective-permute-start.8
  202.1 21.5 %collective-permute-start.9 = (f32[5,128,128]{2,1,0:T(8,128)S(1)}, f32[5,128,128]{2,1,0:T(8,128)S(1)}, u32[]{:S(2)}, u32[]{:S(2)}) collective-permute-start(f32[5,128,128]{2,1,0:T(8,128)S(1)} %fusion.13), channel_id=1, source_target_pairs={{0,0},{1,8},{2,16},{3,24},{4,32},{5,40},{6,48},{7,56},{8,1},{9,9},... | collective-permute-start | bytes 983048 | tf_op jit(solution)/shard_map/ppermute | solution.py:417
  223.6 21.2 %collective-permute-start.10 = (f32[5,128,128]{2,1,0:T(8,128)S(1)}, f32[5,128,128]{2,1,0:T(8,128)S(1)}, u32[]{:S(2)}, u32[]{:S(2)}) collective-permute-start(f32[5,128,128]{2,1,0:T(8,128)S(1)} %collective-permute-done.9), channel_id=1, source_target_pairs={{0,64},{64,0},{1,65},{65,1},{2,66},{66,2},{3,67},{67,3},{4,68},{68... | collective-permute-start | bytes 983048 | tf_op jit(solution)/shard_map/ppermute | solution.py:292
  248.4 33.2 %collective-permute-start.11 = (f32[2,5,128,128]{3,2,1,0:T(8,128)}, f32[2,5,128,128]{3,2,1,0:T(8,128)}, u32[]{:S(2)}, u32[]{:S(2)}) collective-permute-start(f32[2,5,128,128]{3,2,1,0:T(8,128)} %broadcast_select_fusion.3), channel_id=1, source_target_pairs={{0,8},{8,0},{1,9},{9,1},{2,10},{10,2},{3,11},{11,3},{4,12},{12,4},... | collective-permute-start | bytes 1966088 | tf_op jit(solution)/shard_map/ppermute | solution.py:292
  276.0 286.0 %all-to-all-start.2 = ((f32[16,9,128,128]{3,2,1,0:T(8,128)}), f32[16,9,128,128]{3,2,1,0:T(8,128)}, u32[]{:S(2)}, u32[]{:S(2)}) async-start(f32[16,9,128,128]{3,2,1,0:T(8,128)} %place_updates.1), calls=%async_computation.2 | async-start | bytes 18874368 | tf_op jit(solution)/shard_map/all_to_all | solution.py:288
  280.7 259.2 %all-gather.5.cloned.1.call-start = ((), (), s32[]{:S(2)}) async-start(), calls=%async_computation.4 | async-start | bytes 2949120 | tf_op jit(solution)/shard_map/all_gather | solution.py:415
  288.4 56.9 %copy-start.6 = (f32[2,2,5,128,128]{4,3,2,1,0:T(8,128)S(1)}, f32[2,2,5,128,128]{4,3,2,1,0:T(8,128)}, u32[]{:S(2)}) copy-start(f32[2,2,5,128,128]{4,3,2,1,0:T(8,128)} %gather_fusion.6) | copy-start | bytes 3932164
  288.4 171.8 %collective-permute-start.14 = (f32[2,2,5,128,128]{4,3,2,1,0:T(8,128)S(1)}, f32[2,2,5,128,128]{4,3,2,1,0:T(8,128)S(1)}, u32[]{:S(2)}, u32[]{:S(2)}) collective-permute-start(f32[2,2,5,128,128]{4,3,2,1,0:T(8,128)S(1)} %broadcast_select_fusion), channel_id=1, source_target_pairs={{0,48},{16,0},{32,16},{48,32},{1,49},{17,1},{33,17},{49,33},{2,50}... | collective-permute-start | bytes 3932168 | tf_op jit(solution)/shard_map/ppermute | solution.py:292
  289.1 196.8 %collective-permute-start.13 = (f32[2,2,5,128,128]{4,3,2,1,0:T(8,128)S(1)}, f32[2,2,5,128,128]{4,3,2,1,0:T(8,128)S(1)}, u32[]{:S(2)}, u32[]{:S(2)}) collective-permute-start(f32[2,2,5,128,128]{4,3,2,1,0:T(8,128)S(1)} %broadcast_select_fusion), channel_id=1, source_target_pairs={{0,32},{16,48},{32,0},{48,16},{1,33},{17,49},{33,1},{49,17},{2,34}... | collective-permute-start | bytes 3932168 | tf_op jit(solution)/shard_map/ppermute | solution.py:292
  289.9 198.8 %collective-permute-start.12 = (f32[2,2,5,128,128]{4,3,2,1,0:T(8,128)S(1)}, f32[2,2,5,128,128]{4,3,2,1,0:T(8,128)S(1)}, u32[]{:S(2)}, u32[]{:S(2)}) collective-permute-start(f32[2,2,5,128,128]{4,3,2,1,0:T(8,128)S(1)} %broadcast_select_fusion), channel_id=1, source_target_pairs={{0,16},{16,32},{32,48},{48,0},{1,17},{17,33},{33,49},{49,1},{2,18}... | collective-permute-start | bytes 3932168 | tf_op jit(solution)/shard_map/ppermute | solution.py:292
  (10 other events, 30.2 us)
Sparse Core Ops, SparseCore 0:
  12.0 109.6 all-gather.2
  283.2 31.7 all-gather.4
